TPU v7x, 32 devices: a whole 2x2x4 slice. The times are simulated.
32 devices in a mesh: blk: 8 (over z, y), tok: 4 (over x, core).
Axes of the slice: x: 2, y: 2, z: 4, core: 2. Of those that a mesh axis runs over, the one named last changes fastest.
Arguments:
- queries: bfloat16 [256, 32, 128], P('blk'), may hold values from -0.5 to 0.5
- candidates: int32 [256, 4], P('blk'), may hold values from 0 to 7, all different within a row; in each aligned block of 32 rows (0 to 31, 32 to 63, ...) at most 32 rows name the same one
- passages: bfloat16 [8, 180, 32, 128], P('blk', 'tok'), may hold values from -0.5 to 0.5
- lengths: int32 [8, 32], P('blk'), may hold values from 1 to 180
Outputs:
- maxsim: float32 [256, 4, 32], P('blk', None, 'tok')
Inputs may be any that keep to these rules, and one draw needn't show every extreme that they name: `candidates`: each row names 4 different blocks. Among the rows of one index of blk no block is named more than 32 times, and in every draw some block is named exactly 32 times by the rows of some index.
All inputs are finite; a program needn't handle non-finite values.
Results may differ from a plain program's by a relative error of at most 0.0003.
Values may be sent and summed in bfloat16 or wider, within the bound.
A program may use at most 64 MiB of HBM per device.

v0:
```python
import math

import jax
import jax.numpy as jnp
from jax import lax
from jax.sharding import PartitionSpec as P

NEGATIVE_FILL = -1e30


def block_maxima(query_rows, passage, valid_mask, piece_len):
    local_len = passage.shape[0]
    pass_width = passage.shape[1]
    pieces = local_len // piece_len

    def one_piece(step_idx, running):
        offset = step_idx * piece_len
        segment = lax.dynamic_slice_in_dim(passage, offset, piece_len, 0)
        kept_mask = lax.dynamic_slice_in_dim(valid_mask, offset, piece_len, 0)
        flattened = segment.reshape(piece_len * pass_width, segment.shape[2])
        scores = lax.dot_general(
            query_rows, flattened, (((1,), (1,)), ((), ())), preferred_element_type=jnp.float32
        )
        scores = scores.reshape(query_rows.shape[0], piece_len, pass_width)
        scores = jnp.where(kept_mask[None], scores, NEGATIVE_FILL)
        return jnp.maximum(running, jnp.max(scores, axis=1))

    start_max = jnp.full((query_rows.shape[0], pass_width), NEGATIVE_FILL, jnp.float32)
    return lax.fori_loop(0, pieces, one_piece, start_max)


def shards(queries, candidates, passages, lengths):
    num_owners = lax.axis_size("blk")
    num_parts = lax.axis_size("tok")
    part_idx = lax.axis_index("tok")
    query_count, query_len, dim_width = queries.shape
    cand_count = candidates.shape[1]
    pass_width = passages.shape[2]
    part_width = pass_width // num_parts
    capacity = 2 * query_count * cand_count // num_owners
    pair_count = query_count * cand_count
    owner_ids = candidates.reshape(pair_count)
    one_hot = (owner_ids[:, None] == jnp.arange(num_owners, dtype=jnp.int32)[None, :]).astype(
        jnp.int32
    )
    earlier = jnp.cumsum(one_hot, axis=0) - one_hot
    position = jnp.sum(earlier * one_hot, axis=1)
    slot_ids = owner_ids * capacity + position
    dispatch = (
        jnp.arange(num_owners * capacity, dtype=jnp.int32)[:, None] == slot_ids[None, :]
    ).astype(jnp.bfloat16)
    repeated = jnp.repeat(queries.reshape(query_count, query_len * dim_width), cand_count, axis=0)
    outgoing = jnp.dot(dispatch, repeated, preferred_element_type=jnp.float32).astype(jnp.bfloat16)
    outgoing = outgoing.reshape(num_owners, capacity, query_len, dim_width)
    moved = lax.all_to_all(passages, "tok", split_axis=2, concat_axis=1, tiled=True)
    passage = moved[0]
    own_lengths = lax.dynamic_slice_in_dim(lengths[0], part_idx * part_width, part_width, 0)
    token_pos = jnp.arange(passage.shape[0], dtype=jnp.int32)
    valid_mask = token_pos[:, None] < own_lengths[None, :]
    score_len = passage.shape[0]
    score_width = passage.shape[1]
    piece_len = max((divisor for divisor in range(1, 17) if score_len % divisor == 0))
    received = lax.all_to_all(outgoing, "blk", split_axis=0, concat_axis=0, tiled=True)
    senders = received.shape[0]
    item_count = received.shape[1]
    slot_total = senders * item_count
    group_size = math.gcd(slot_total, 16)
    grouped = received.reshape(slot_total // group_size, group_size * query_len, dim_width)

    def per_group(query_rows):
        return block_maxima(query_rows, passage, valid_mask, piece_len)

    maxima = lax.map(per_group, grouped).reshape(senders, item_count, query_len, score_width)
    totals = jnp.sum(maxima, axis=2)
    returned = lax.all_to_all(totals, "blk", split_axis=0, concat_axis=0, tiled=True)
    flat_scores = returned.reshape(num_owners * capacity, part_width)
    picked = jnp.take(flat_scores, slot_ids, axis=0)
    return picked.reshape(query_count, cand_count, part_width)


def solution(mesh):
    in_specs = (P("blk", None, None), P("blk", None), P("blk", "tok", None, None), P("blk", None))
    out_specs = P("blk", None, "tok")
    return jax.shard_map(shards, mesh=mesh, in_specs=in_specs, out_specs=out_specs, check_vma=False)
```

profile of v0, /device:TPU:0, one launch (start us, length us, event | category | flops | bytes accessed | tf_op | source)
XLA Modules:
  0.0 142.6 jit_solution(10993279197498296157)
XLA Ops:
  0.0 1.9 %copy.27 = bf16[1,45,32,128]{3,1,0,2:T(8,128)(2,1)} copy(bf16[1,45,32,128]{3,2,1,0:T(8,128)(2,1)} %param.10) | data formatting | bytes 737280 | tf_op args[2]
  1.9 4.2 %all-to-all-start.1 = ((bf16[1,45,32,128]{3,1,0,2:T(8,128)(2,1)}), bf16[1,45,32,128]{3,1,0,2:T(8,128)(2,1)S(1)}, u32[]{:S(2)}, u32[]{:S(2)}) async-start(bf16[1,45,32,128]{3,1,0,2:T(8,128)(2,1)} %copy.27), calls=%async_computation.1 | async-start | bytes 786432 | tf_op jit(solution)/shard_map/all_to_all | solution.py:55
  10.0 1.8 %copy.38 = bf16[32,8,32,128]{3,2,1,0:T(8,128)(2,1)} copy(bf16[32,8,32,128]{3,1,2,0:T(8,128)(2,1)S(1)} %fusion.7) | data formatting | bytes 4194304
  13.6 6.6 %all-to-all-start = ((bf16[8,32,32,128]{3,2,1,0:T(8,128)(2,1)}), bf16[8,32,32,128]{3,2,1,0:T(8,128)(2,1)S(1)}, u32[]{:S(2)}, u32[]{:S(2)}) async-start(bf16[8,32,32,128]{3,2,1,0:T(8,128)(2,1)} %bitcast.20), calls=%async_computation | async-start | bytes 4194304 | tf_op jit(solution)/shard_map/all_to_all | solution.py:63
  20.8 47.4 %all-to-all-done = bf16[8,32,32,128]{3,2,1,0:T(8,128)(2,1)S(1)} async-done(((bf16[8,32,32,128]{3,2,1,0:T(8,128)(2,1)}), bf16[8,32,32,128]{3,2,1,0:T(8,128)(2,1)S(1)}, u32[]{:S(2)}, u32[]{:S(2)}) %all-to-all-start) | async-done | bytes 2097184 | tf_op jit(solution)/shard_map/all_to_all | solution.py:63
  68.2 60.2 %while.27 = (s32[]{:T(128)}, f32[16,512,8]{1,0,2:T(8,128)S(1)}, bf16[16,512,128]{2,1,0:T(8,128)(2,1)S(1)}, bf16[180,8,128]{2,1,0:T(8,128)(2,1)S(1)}, s32[8]{0:T(...) while((s32[]{:T(128)}, f32[16,512,8]{1,0,2:T(8,128)S(1)}, ...), condition=%wide.region_6.7_spmd.clone, body=%wide.region_2.6_spmd.clone.sunk | while | flops 15857065 | bytes 559122 | solution.py:73
  68.3 3.5 %while.28 = (s32[]{:T(128)}, f32[512,8]{0,1:T(8,128)S(1)}, pred[180,8]{1,0:T(8,128)(4,1)S(1)}, bf16[180,8,128]{2,1,0:T(8,128)(2,1)S(1)}, bf16[512,128]{1,0:T(8,1...) while((s32[]{:T(128)}, f32[512,8]{0,1:T(8,128)S(1)}, ...), condition=%wide.region_5.5_spmd.clone, body=%wide.region_3.4_spmd.clone.sunk | while | flops 15855623 | bytes 229773 | solution.py:29
  72.1 3.5 %while.28 = (s32[]{:T(128)}, f32[512,8]{0,1:T(8,128)S(1)}, pred[180,8]{1,0:T(8,128)(4,1)S(1)}, bf16[180,8,128]{2,1,0:T(8,128)(2,1)S(1)}, bf16[512,128]{1,0:T(8,1...) while((s32[]{:T(128)}, f32[512,8]{0,1:T(8,128)S(1)}, ...), condition=%wide.region_5.5_spmd.clone, body=%wide.region_3.4_spmd.clone.sunk | while | flops 15855623 | bytes 229773 | solution.py:29
  75.8 3.5 %while.28 = (s32[]{:T(128)}, f32[512,8]{0,1:T(8,128)S(1)}, pred[180,8]{1,0:T(8,128)(4,1)S(1)}, bf16[180,8,128]{2,1,0:T(8,128)(2,1)S(1)}, bf16[512,128]{1,0:T(8,1...) while((s32[]{:T(128)}, f32[512,8]{0,1:T(8,128)S(1)}, ...), condition=%wide.region_5.5_spmd.clone, body=%wide.region_3.4_spmd.clone.sunk | while | flops 15855623 | bytes 229773 | solution.py:29
  79.6 3.5 %while.28 = (s32[]{:T(128)}, f32[512,8]{0,1:T(8,128)S(1)}, pred[180,8]{1,0:T(8,128)(4,1)S(1)}, bf16[180,8,128]{2,1,0:T(8,128)(2,1)S(1)}, bf16[512,128]{1,0:T(8,1...) while((s32[]{:T(128)}, f32[512,8]{0,1:T(8,128)S(1)}, ...), condition=%wide.region_5.5_spmd.clone, body=%wide.region_3.4_spmd.clone.sunk | while | flops 15855623 | bytes 229773 | solution.py:29
  83.4 3.5 %while.28 = (s32[]{:T(128)}, f32[512,8]{0,1:T(8,128)S(1)}, pred[180,8]{1,0:T(8,128)(4,1)S(1)}, bf16[180,8,128]{2,1,0:T(8,128)(2,1)S(1)}, bf16[512,128]{1,0:T(8,1...) while((s32[]{:T(128)}, f32[512,8]{0,1:T(8,128)S(1)}, ...), condition=%wide.region_5.5_spmd.clone, body=%wide.region_3.4_spmd.clone.sunk | while | flops 15855623 | bytes 229773 | solution.py:29
  87.1 3.5 %while.28 = (s32[]{:T(128)}, f32[512,8]{0,1:T(8,128)S(1)}, pred[180,8]{1,0:T(8,128)(4,1)S(1)}, bf16[180,8,128]{2,1,0:T(8,128)(2,1)S(1)}, bf16[512,128]{1,0:T(8,1...) while((s32[]{:T(128)}, f32[512,8]{0,1:T(8,128)S(1)}, ...), condition=%wide.region_5.5_spmd.clone, body=%wide.region_3.4_spmd.clone.sunk | while | flops 15855623 | bytes 229773 | solution.py:29
  90.9 3.5 %while.28 = (s32[]{:T(128)}, f32[512,8]{0,1:T(8,128)S(1)}, pred[180,8]{1,0:T(8,128)(4,1)S(1)}, bf16[180,8,128]{2,1,0:T(8,128)(2,1)S(1)}, bf16[512,128]{1,0:T(8,1...) while((s32[]{:T(128)}, f32[512,8]{0,1:T(8,128)S(1)}, ...), condition=%wide.region_5.5_spmd.clone, body=%wide.region_3.4_spmd.clone.sunk | while | flops 15855623 | bytes 229773 | solution.py:29
  94.7 3.5 %while.28 = (s32[]{:T(128)}, f32[512,8]{0,1:T(8,128)S(1)}, pred[180,8]{1,0:T(8,128)(4,1)S(1)}, bf16[180,8,128]{2,1,0:T(8,128)(2,1)S(1)}, bf16[512,128]{1,0:T(8,1...) while((s32[]{:T(128)}, f32[512,8]{0,1:T(8,128)S(1)}, ...), condition=%wide.region_5.5_spmd.clone, body=%wide.region_3.4_spmd.clone.sunk | while | flops 15855623 | bytes 229773 | solution.py:29
  98.4 3.5 %while.28 = (s32[]{:T(128)}, f32[512,8]{0,1:T(8,128)S(1)}, pred[180,8]{1,0:T(8,128)(4,1)S(1)}, bf16[180,8,128]{2,1,0:T(8,128)(2,1)S(1)}, bf16[512,128]{1,0:T(8,1...) while((s32[]{:T(128)}, f32[512,8]{0,1:T(8,128)S(1)}, ...), condition=%wide.region_5.5_spmd.clone, body=%wide.region_3.4_spmd.clone.sunk | while | flops 15855623 | bytes 229773 | solution.py:29
  102.2 3.5 %while.28 = (s32[]{:T(128)}, f32[512,8]{0,1:T(8,128)S(1)}, pred[180,8]{1,0:T(8,128)(4,1)S(1)}, bf16[180,8,128]{2,1,0:T(8,128)(2,1)S(1)}, bf16[512,128]{1,0:T(8,1...) while((s32[]{:T(128)}, f32[512,8]{0,1:T(8,128)S(1)}, ...), condition=%wide.region_5.5_spmd.clone, body=%wide.region_3.4_spmd.clone.sunk | while | flops 15855623 | bytes 229773 | solution.py:29
  105.9 3.5 %while.28 = (s32[]{:T(128)}, f32[512,8]{0,1:T(8,128)S(1)}, pred[180,8]{1,0:T(8,128)(4,1)S(1)}, bf16[180,8,128]{2,1,0:T(8,128)(2,1)S(1)}, bf16[512,128]{1,0:T(8,1...) while((s32[]{:T(128)}, f32[512,8]{0,1:T(8,128)S(1)}, ...), condition=%wide.region_5.5_spmd.clone, body=%wide.region_3.4_spmd.clone.sunk | while | flops 15855623 | bytes 229773 | solution.py:29
  109.7 3.5 %while.28 = (s32[]{:T(128)}, f32[512,8]{0,1:T(8,128)S(1)}, pred[180,8]{1,0:T(8,128)(4,1)S(1)}, bf16[180,8,128]{2,1,0:T(8,128)(2,1)S(1)}, bf16[512,128]{1,0:T(8,1...) while((s32[]{:T(128)}, f32[512,8]{0,1:T(8,128)S(1)}, ...), condition=%wide.region_5.5_spmd.clone, body=%wide.region_3.4_spmd.clone.sunk | while | flops 15855623 | bytes 229773 | solution.py:29
  113.5 3.5 %while.28 = (s32[]{:T(128)}, f32[512,8]{0,1:T(8,128)S(1)}, pred[180,8]{1,0:T(8,128)(4,1)S(1)}, bf16[180,8,128]{2,1,0:T(8,128)(2,1)S(1)}, bf16[512,128]{1,0:T(8,1...) while((s32[]{:T(128)}, f32[512,8]{0,1:T(8,128)S(1)}, ...), condition=%wide.region_5.5_spmd.clone, body=%wide.region_3.4_spmd.clone.sunk | while | flops 15855623 | bytes 229773 | solution.py:29
  117.2 3.5 %while.28 = (s32[]{:T(128)}, f32[512,8]{0,1:T(8,128)S(1)}, pred[180,8]{1,0:T(8,128)(4,1)S(1)}, bf16[180,8,128]{2,1,0:T(8,128)(2,1)S(1)}, bf16[512,128]{1,0:T(8,1...) while((s32[]{:T(128)}, f32[512,8]{0,1:T(8,128)S(1)}, ...), condition=%wide.region_5.5_spmd.clone, body=%wide.region_3.4_spmd.clone.sunk | while | flops 15855623 | bytes 229773 | solution.py:29
  121.0 3.5 %while.28 = (s32[]{:T(128)}, f32[512,8]{0,1:T(8,128)S(1)}, pred[180,8]{1,0:T(8,128)(4,1)S(1)}, bf16[180,8,128]{2,1,0:T(8,128)(2,1)S(1)}, bf16[512,128]{1,0:T(8,1...) while((s32[]{:T(128)}, f32[512,8]{0,1:T(8,128)S(1)}, ...), condition=%wide.region_5.5_spmd.clone, body=%wide.region_3.4_spmd.clone.sunk | while | flops 15855623 | bytes 229773 | solution.py:29
  124.8 3.5 %while.28 = (s32[]{:T(128)}, f32[512,8]{0,1:T(8,128)S(1)}, pred[180,8]{1,0:T(8,128)(4,1)S(1)}, bf16[180,8,128]{2,1,0:T(8,128)(2,1)S(1)}, bf16[512,128]{1,0:T(8,1...) while((s32[]{:T(128)}, f32[512,8]{0,1:T(8,128)S(1)}, ...), condition=%wide.region_5.5_spmd.clone, body=%wide.region_3.4_spmd.clone.sunk | while | flops 15855623 | bytes 229773 | solution.py:29
  129.8 3.6 %all-to-all-start.2 = ((f32[8,1,256]{2,1,0:T(1,128)}), f32[8,1,256]{2,1,0:T(1,128)S(1)}, u32[]{:S(2)}, u32[]{:S(2)}) async-start(f32[8,1,256]{2,1,0:T(1,128)} %reshape.107), calls=%async_computation.2 | async-start | bytes 16384 | tf_op jit(solution)/shard_map/all_to_all | solution.py:75
  133.4 6.5 %all-to-all-done.2 = f32[8,1,256]{2,1,0:T(1,128)S(1)} async-done(((f32[8,1,256]{2,1,0:T(1,128)}), f32[8,1,256]{2,1,0:T(1,128)S(1)}, u32[]{:S(2)}, u32[]{:S(2)}) %all-to-all-start.2) | async-done | bytes 8224 | tf_op jit(solution)/shard_map/all_to_all | solution.py:75
  (693 shorter events, 60.4 us)
Async XLA Ops:
  0.0 20.6 %copy-start = (s32[1,32]{1,0:T(1,128)S(1)}, s32[1,32]{1,0:T(1,128)}, u32[]{:S(2)}) copy-start(s32[1,32]{1,0:T(1,128)} %param.11) | copy-start | bytes 388
  1.9 11.7 %all-to-all-start.1 = ((bf16[1,45,32,128]{3,1,0,2:T(8,128)(2,1)}), bf16[1,45,32,128]{3,1,0,2:T(8,128)(2,1)S(1)}, u32[]{:S(2)}, u32[]{:S(2)}) async-start(bf16[1,45,32,128]{3,1,0,2:T(8,128)(2,1)} %copy.27), calls=%async_computation.1 | async-start | bytes 786432 | tf_op jit(solution)/shard_map/all_to_all | solution.py:55
  13.6 6.7 %copy-start.1 = (s32[32,4]{0,1:T(4,128)S(1)}, s32[32,4]{0,1:T(4,128)}, u32[]{:S(2)}) copy-start(s32[32,4]{0,1:T(4,128)} %param.9) | copy-start | bytes 1540
  13.6 54.7 %all-to-all-start = ((bf16[8,32,32,128]{3,2,1,0:T(8,128)(2,1)}), bf16[8,32,32,128]{3,2,1,0:T(8,128)(2,1)S(1)}, u32[]{:S(2)}, u32[]{:S(2)}) async-start(bf16[8,32,32,128]{3,2,1,0:T(8,128)(2,1)} %bitcast.20), calls=%async_computation | async-start | bytes 4194304 | tf_op jit(solution)/shard_map/all_to_all | solution.py:63
  129.8 10.1 %all-to-all-start.2 = ((f32[8,1,256]{2,1,0:T(1,128)}), f32[8,1,256]{2,1,0:T(1,128)S(1)}, u32[]{:S(2)}, u32[]{:S(2)}) async-start(f32[8,1,256]{2,1,0:T(1,128)} %reshape.107), calls=%async_computation.2 | async-start | bytes 16384 | tf_op jit(solution)/shard_map/all_to_all | solution.py:75
where the time goes:
time: 143 us
  waiting for transfers between devices  55.7 us (39%)
  matrix products  43.6 us (30%)
  local copies, waits for them, and re-layouts  15.1 us (11%)
  starting transfers between devices  14.5 us (10%)
  loops' own time  9.94 us (7%)
  other arithmetic  3.77 us (3%)
    all_to_all x1, waiting for transfers between devices, shards(): lax.all_to_all(outgoing, 'blk', split_axis=0, concat_axis=0, tiled=True)  47.4 us
    dot_general x192, matrix products, one_piece(): lax.dot_general(query_rows, flattened, (((1,), (1,)), ((), ())), preferre...  42.9 us
    another operation x16, loops' own time, block_maxima(): return lax.fori_loop(0, pieces, one_piece, start_max)  8.98 us
    all_to_all x1, starting transfers between devices, shards(): lax.all_to_all(outgoing, 'blk', split_axis=0, concat_axis=0, tiled=True)  6.64 us
    all_to_all x1, waiting for transfers between devices, shards(): lax.all_to_all(totals, 'blk', split_axis=0, concat_axis=0, tiled=True)  6.51 us
    unnamed x10, local copies, waits for them, and re-layouts  6.34 us
    all_to_all x1, starting transfers between devices, shards(): lax.all_to_all(passages, 'tok', split_axis=2, concat_axis=1, tiled=True)  4.21 us
    all_to_all x1, starting transfers between devices, shards(): lax.all_to_all(totals, 'blk', split_axis=0, concat_axis=0, tiled=True)  3.63 us
  transfers between devices with their start and end apart: 3, of which 3 were waited for; matrix products, arithmetic and copies ran while one was open for 4% of the time, Pallas kernels for 0%

commit v1 on v0

--- a/solution.py
+++ b/solution.py
@@ -1,8 +1,11 @@
+import functools
 import math
 
 import jax
 import jax.numpy as jnp
 from jax import lax
+from jax.experimental import pallas as pl
+from jax.experimental.pallas import tpu as pltpu
 from jax.sharding import PartitionSpec as P
 
 NEGATIVE_FILL = -1e30
@@ -29,7 +32,7 @@
     return lax.fori_loop(0, pieces, one_piece, start_max)
 
 
-def shards(queries, candidates, passages, lengths):
+def dispatch_shards(queries, candidates, passages, lengths):
     num_owners = lax.axis_size("blk")
     num_parts = lax.axis_size("tok")
     part_idx = lax.axis_index("tok")
@@ -40,11 +43,9 @@
     capacity = 2 * query_count * cand_count // num_owners
     pair_count = query_count * cand_count
     owner_ids = candidates.reshape(pair_count)
-    one_hot = (owner_ids[:, None] == jnp.arange(num_owners, dtype=jnp.int32)[None, :]).astype(
-        jnp.int32
-    )
-    earlier = jnp.cumsum(one_hot, axis=0) - one_hot
-    position = jnp.sum(earlier * one_hot, axis=1)
+    pair_ids = jnp.arange(pair_count, dtype=jnp.int32)
+    same = (owner_ids[:, None] == owner_ids[None, :]) & (pair_ids[None, :] < pair_ids[:, None])
+    position = jnp.sum(same.astype(jnp.int32), axis=1)
     slot_ids = owner_ids * capacity + position
     dispatch = (
         jnp.arange(num_owners * capacity, dtype=jnp.int32)[:, None] == slot_ids[None, :]
@@ -78,7 +79,357 @@
     return picked.reshape(query_count, cand_count, part_width)
 
 
+LANES = 128
+SUB = 8
+MESH = pl.DeviceIdType.MESH
+
+
+def dense_kernel(
+    owners, parts, width, q_len, chunks,
+    p_ref, q_ref, len_ref, cand_ref, out_ref,
+    p_all, p_fix, p_first, q_all, acc, r_out, r_in,
+    q_send, q_recv, near_send, near_recv, far_send, far_recv, hop_send, hop_recv,
+    first_send, first_recv, r_send, r_recv,
+):
+    slots = p_ref.shape[0]
+    piece = slots // chunks
+    cols = q_len and q_all.shape[1]
+    tiles = cols // LANES
+    cand_count = cand_ref.shape[0]
+    depth = owners // 2
+    me, part = lax.axis_index("blk"), lax.axis_index("tok")
+    z, y = me // 2, me % 2
+    across, core = part // 2, part % 2
+    partner = across * 2 + 1 - core
+    opposite = (1 - across) * 2 + core
+    diagonal = (1 - across) * 2 + 1 - core
+
+    def remote(src, dst, send, recv, blk, tok):
+        return pltpu.make_async_remote_copy(
+            src_ref=src, dst_ref=dst, send_sem=send, recv_sem=recv,
+            device_id={"blk": blk, "tok": tok}, device_id_type=MESH,
+        )
+
+    own_q = pltpu.make_async_copy(q_ref.at[part], q_all.at[me], q_recv.at[me])
+    own_p = pltpu.make_async_copy(p_ref, p_all.at[0], near_recv.at[0])
+    own_q.start()
+    own_p.start()
+
+    barrier = pltpu.get_barrier_semaphore()
+    total = owners * parts
+    flat = me * parts + part
+
+    def greet(i, carry):
+        other = (flat + i) % total
+        pl.semaphore_signal(
+            barrier, inc=1, device_id={"blk": other // parts, "tok": other % parts},
+            device_id_type=MESH,
+        )
+        return carry
+
+    lax.fori_loop(1, total, greet, 0)
+    pl.semaphore_wait(barrier, total - 1)
+
+    def q_copy(src, slot, way, blk):
+        return remote(src, q_all.at[slot], q_send.at[slot, way], q_recv.at[slot], blk, part)
+
+    def first_copy(j):
+        return remote(
+            p_ref.at[0], p_first, first_send.at[j], first_recv, me, (part + j) % parts
+        )
+
+    first_own = pltpu.make_async_copy(p_ref.at[0], p_first, first_recv)
+
+    def far_copy(i):
+        rows = pl.ds(i * piece, piece)
+        return remote(
+            p_ref.at[rows], p_all.at[2, rows], far_send.at[i], far_recv.at[i], me, opposite
+        )
+
+    def hop_copy(i):
+        rows = pl.ds(i * piece, piece)
+        return remote(
+            p_all.at[2, rows], p_all.at[3, rows], hop_send.at[i], hop_recv.at[i], me, partner
+        )
+
+    near = remote(p_ref, p_all.at[1], near_send, near_recv.at[1], me, partner)
+
+    def beside(slot, src):
+        return q_copy(src, slot, 0, z * 2 + 1 - y)
+
+    def along(slot, src, to_z):
+        return q_copy(src, slot, 1, to_z * 2 + y)
+
+    def along_down(slot, src):
+        return q_copy(src, slot, 2, (z - 1) * 2 + y)
+
+    @pl.when(part == 0)
+    def _():
+        first_own.start()
+        for j in range(1, parts):
+            first_copy(j).start()
+
+    beside(me, q_ref.at[part]).start()
+
+    @pl.when(z + 1 < depth)
+    def _():
+        along(me, q_ref.at[part], z + 1).start()
+
+    @pl.when(z > 0)
+    def _():
+        along_down(me, q_ref.at[part]).start()
+
+    near.start()
+    for i in range(chunks):
+        far_copy(i).start()
+
+    def source(k):
+        both = jnp.minimum(z, depth - 1 - z)
+        paired = k <= 2 * both
+        sign = jnp.where(
+            paired, jnp.where(k % 2 == 1, -1, 1), jnp.where(z <= depth - 1 - z, 1, -1)
+        )
+        far = jnp.where(paired, (k + 1) // 2, k - both)
+        return z + sign * far
+
+    last = owners - 1
+
+    def is_column(n):
+        return (n == 0) | ((n % 2 == 1) & (n < last))
+
+    def slot_of(n):
+        k = jnp.where(n == last, depth - 1, jnp.where(n % 2 == 1, (n + 1) // 2, n // 2 - 1))
+        k = jnp.where(n == 0, 0, k)
+        return source(k) * 2 + jnp.where(is_column(n), y, 1 - y)
+
+    def fix(place, tok):
+        pos = lax.broadcasted_iota(jnp.int32, (slots, width, LANES), 0) + tok * slots
+        kept = pos < len_ref[...][None]
+        mine = p_all[place].astype(jnp.float32)
+        first = p_first[...].astype(jnp.float32)
+        p_fix[place] = jnp.where(kept, mine, first[None]).astype(p_fix.dtype)
+
+    def best(slot, place):
+        rows = p_fix[place].reshape(slots * width, LANES)
+        scores = lax.dot_general(
+            rows, q_all[slot], (((1,), (1,)), ((), ())), preferred_element_type=jnp.float32
+        )
+        return jnp.max(scores.reshape(slots, width, cols), axis=0)
+
+    first_own.wait()
+    own_p.wait()
+    fix(0, part)
+    near.wait_recv()
+    fix(1, partner)
+
+    def onward(n):
+        slot = slot_of(n)
+        from_z = slot // 2
+        src = q_all.at[slot]
+        up = (from_z < z) & (z + 1 < depth)
+        down = (from_z > z) & (z > 0)
+        return slot, src, up, down
+
+    def early(n, carry):
+        slot, src, up, down = onward(n)
+        pltpu.make_async_copy(src, src, q_recv.at[slot]).wait()
+
+        @pl.when(is_column(n) & (n > 0))
+        def _():
+            beside(slot, src).start()
+
+            @pl.when(up)
+            def _():
+                along(slot, src, z + 1).start()
+
+            @pl.when(down)
+            def _():
+                along_down(slot, src).start()
+
+        for i in range(chunks):
+
+            @pl.when(n == 2 * i + 2)
+            def _():
+                far_copy(i).wait_recv()
+                hop_copy(i).start()
+
+        acc[n] = jnp.maximum(best(slot, 0), best(slot, 1))
+        return carry
+
+    lax.fori_loop(0, owners, early, 0)
+
+    for i in range(chunks):
+        hop_copy(i).wait_recv()
+    fix(2, opposite)
+    fix(3, diagonal)
+
+    lane = lax.broadcasted_iota(jnp.int32, (SUB, LANES), 1)
+
+    def r_copy(slot, j):
+        tok = (part + j) % parts
+        return remote(
+            r_out.at[slot], r_in.at[me, part], r_send.at[slot, tok], r_recv.at[me, part], slot, tok
+        )
+
+    def late(n, carry):
+        slot = slot_of(n)
+        found = jnp.maximum(acc[n], jnp.maximum(best(slot, 2), best(slot, 3)))
+        tile = jnp.zeros((SUB, LANES), jnp.float32)
+        for g in range(tiles):
+            sums = found[:, g * LANES : (g + 1) * LANES]
+            step = q_len // 2
+            while step:
+                sums = sums + pltpu.roll(sums, LANES - step, 1)
+                step //= 2
+            for group in range(parts):
+                at = group * tiles + g
+                piece_sums = sums[group * SUB : (group + 1) * SUB]
+                if at:
+                    piece_sums = pltpu.roll(piece_sums, at, 1)
+                tile = jnp.where(lane % q_len == at, piece_sums, tile)
+        r_out[slot] = tile
+        for j in range(1, parts):
+            r_copy(slot, j).start()
+
+        @pl.when(n > 0)
+        def _():
+            r_copy(slot, 0).start()
+
+        @pl.when(n == 0)
+        def _():
+            r_in[me, part] = tile
+
+        return carry
+
+    lax.fori_loop(0, owners, late, 0)
+
+    def drain(n, carry):
+        slot, src, up, down = onward(n)
+
+        @pl.when(is_column(n))
+        def _():
+            beside(slot, src).wait_send()
+
+            @pl.when(up | ((n == 0) & (z + 1 < depth)))
+            def _():
+                along(slot, src, z + 1).wait_send()
+
+            @pl.when(down | ((n == 0) & (z > 0)))
+            def _():
+                along_down(slot, src).wait_send()
+
+        for j in range(parts):
+
+            @pl.when((n > 0) | (j > 0))
+            def _():
+                tok = (part + j) % parts
+                r_copy(slot, j).wait_send()
+                here = r_in.at[slot, tok]
+                pltpu.make_async_copy(here, here, r_recv.at[slot, tok]).wait()
+
+        return carry
+
+    lax.fori_loop(0, owners, drain, 0)
+    near.wait_send()
+    for i in range(chunks):
+        far_copy(i).wait_send()
+        hop_copy(i).wait_send()
+
+    @pl.when(part == 0)
+    def _():
+        for j in range(1, parts):
+            first_copy(j).wait_send()
+
+    picked = [jnp.zeros((SUB, LANES), jnp.float32) for _ in range(cand_count)]
+    for blk in range(owners):
+        merged = jnp.zeros((SUB, LANES), jnp.float32)
+        for tok in range(parts):
+            moved = pltpu.roll(r_in[blk, tok], (tiles * (tok - part) + LANES) % LANES, 1)
+            merged = jnp.where((lane % q_len) // tiles == tok, moved, merged)
+        for k in range(cand_count):
+            picked[k] = jnp.where(cand_ref[k : k + 1, :] == blk, merged, picked[k])
+    for k in range(cand_count):
+        out_ref[k] = picked[k]
+
+
+def dense_shards(queries, candidates, passages, lengths):
+    owners, parts = lax.axis_size("blk"), lax.axis_size("tok")
+    query_count, q_len, dim = queries.shape
+    cand_count = candidates.shape[1]
+    slots, width = passages.shape[1], passages.shape[2]
+    share = query_count // parts
+    cols = share * q_len
+    tiles = cols // LANES
+    per = LANES // q_len
+    chunks = 3 if slots % 3 == 0 else 1
+    used = parts * tiles
+    cand = candidates.reshape(parts, tiles, per, cand_count).transpose(3, 2, 0, 1)
+    cand = cand.reshape(cand_count, per, used)
+    cand = jnp.pad(cand, ((0, 0), (0, 0), (0, q_len - used))).reshape(cand_count, LANES)
+    limits = jnp.broadcast_to(lengths[0][:, None], (width, LANES))
+    dma = pltpu.SemaphoreType.DMA
+    out = pl.pallas_call(
+        functools.partial(dense_kernel, owners, parts, width, q_len, chunks),
+        out_shape=jax.ShapeDtypeStruct((cand_count, SUB, LANES), jnp.float32),
+        in_specs=[pl.BlockSpec(memory_space=pl.ANY)] * 2
+        + [pl.BlockSpec(memory_space=pltpu.VMEM)] * 2,
+        out_specs=pl.BlockSpec(memory_space=pltpu.VMEM),
+        scratch_shapes=[
+            pltpu.VMEM((4, slots, width, dim), passages.dtype),
+            pltpu.VMEM((4, slots, width, dim), passages.dtype),
+            pltpu.VMEM((width, dim), passages.dtype),
+            pltpu.VMEM((owners, cols, dim), queries.dtype),
+            pltpu.VMEM((owners, width, cols), jnp.float32),
+            pltpu.VMEM((owners, SUB, LANES), jnp.float32),
+            pltpu.VMEM((owners, parts, SUB, LANES), jnp.float32),
+            dma((owners, 3)),
+            dma((owners,)),
+            dma,
+            dma((2,)),
+            dma((chunks,)),
+            dma((chunks,)),
+            dma((chunks,)),
+            dma((chunks,)),
+            dma((parts,)),
+            dma,
+            dma((owners, parts)),
+            dma((owners, parts)),
+        ],
+        compiler_params=pltpu.CompilerParams(
+            collective_id=0, has_side_effects=True, vmem_limit_bytes=48 * 1024 * 1024
+        ),
+    )(passages[0], queries.reshape(parts, cols, dim), limits, cand)
+    out = out.reshape(cand_count, SUB, per, q_len)[:, :, :, :used]
+    out = out.reshape(cand_count, SUB, per, parts, tiles).transpose(3, 4, 2, 0, 1)
+    return out.reshape(query_count, cand_count, SUB)
+
+
+def dense_fits(mesh, queries, candidates, passages):
+    owners, parts = mesh.shape["blk"], mesh.shape["tok"]
+    query_count, q_len = queries.shape[0] // owners, queries.shape[1]
+    if owners % 2 or parts != 4 or query_count % parts or LANES % q_len:
+        return False
+    cols = query_count // parts * q_len
+    return (
+        owners <= 4 * candidates.shape[1]
+        and passages.shape[0] == owners
+        and cols % LANES == 0
+        and parts * (cols // LANES) <= q_len
+        and passages.shape[2] == parts * SUB
+        and passages.shape[3] == LANES
+        and passages.shape[1] % parts == 0
+    )
+
+
 def solution(mesh):
     in_specs = (P("blk", None, None), P("blk", None), P("blk", "tok", None, None), P("blk", None))
     out_specs = P("blk", None, "tok")
-    return jax.shard_map(shards, mesh=mesh, in_specs=in_specs, out_specs=out_specs, check_vma=False)
+
+    def run(queries, candidates, passages, lengths):
+        fits = dense_fits(mesh, queries, candidates, passages)
+        body = dense_shards if fits else dispatch_shards
+        return jax.shard_map(
+            body, mesh=mesh, in_specs=in_specs, out_specs=out_specs, check_vma=False
+        )(queries, candidates, passages, lengths)
+
+    return run

time: 143 us -> 40.7 us (0.28)
  waiting for transfers between devices: 55.7 us -> 0 us
  matrix products: 43.6 us -> 0 us
  Pallas kernels: 0 us -> 36.1 us
  starting transfers between devices: 14.5 us -> 0 us
  local copies, waits for them, and re-layouts: 15.1 us -> 4.38 us
  loops' own time: 9.94 us -> 0 us
  other arithmetic: 3.77 us -> 0 us
    all_to_all x3 -> x0, waiting for transfers between devices: 55.7 us -> none  [the longest x1 47.4 us: shards(): lax.all_to_all(outgoing, 'blk', split_axis=0, concat_axis=0, tiled=True)]
    dot_general x193 -> x0, matrix products: 43.6 us -> none  [the longest x192 42.9 us: one_piece(): lax.dot_general(query_rows, flattened, (((1,), (1,)), ((), ())), preferre...]
    pallas_call x0 -> x1, Pallas kernels: none -> 36.1 us  [dense_shards(): pl.pallas_call(functools.partial(dense_kernel, owners, parts, width, q_le...]
    all_to_all x3 -> x0, starting transfers between devices: 14.5 us -> none  [the longest x1 6.64 us: shards(): lax.all_to_all(outgoing, 'blk', split_axis=0, concat_axis=0, tiled=True)]
    another operation x17 -> x0, loops' own time: 9.94 us -> none  [the longest x16 8.98 us: block_maxima(): return lax.fori_loop(0, pieces, one_piece, start_max)]
    dynamic_slice x192 -> x0, local copies, waits for them, and re-layouts: 3.44 us -> none  [one_piece(): kept_mask = lax.dynamic_slice_in_dim(valid_mask, offset, piece_len, 0)]
    unnamed x10 -> x9, local copies, waits for them, and re-layouts: 6.34 us -> 3.29 us
    dynamic_update_slice x32 -> x0, local copies, waits for them, and re-layouts: 2.02 us -> none  [shards(): lax.map(per_group, grouped)]
  transfers between devices with their start and end apart: 3 -> 0, of which waited for: 3 -> 0; matrix products, arithmetic and copies ran while one was open for 4% -> 0% of each run, Pallas kernels for 0% -> 0%
where the time goes in v1:
time: 40.7 us; the launch traced here: 40.5 us
  Pallas kernels  36.1 us (89%)
  local copies, waits for them, and re-layouts  4.38 us (11%)
    pallas_call x1, Pallas kernels, dense_shards(): pl.pallas_call(functools.partial(dense_kernel, owners, parts, width, q_le...  36.1 us
    unnamed x9, local copies, waits for them, and re-layouts  3.29 us

profile of v1, /device:TPU:0, one launch (start us, length us, event | category | flops | bytes accessed | tf_op | source)
XLA Modules:
  0.0 40.5 jit_solution(3874652621522229879)
XLA Ops:
  0.0 0.0 copy-start.2
  0.0 0.7 %copy-done.2 = s32[32,4]{0,1:T(4,128)S(1)} copy-done((s32[32,4]{0,1:T(4,128)S(1)}, s32[32,4]{0,1:T(4,128)}, u32[]{:S(2)}) %copy-start.2) | copy-done | bytes 536
  0.7 0.1 reshape.23
  0.8 0.1 copy.12
  0.9 0.0 copy-start.3
  0.9 0.1 reshape.25.cand_ref
  1.0 0.6 %copy-done.3 = s32[1,32]{1,0:T(1,128)S(1)} copy-done((s32[1,32]{1,0:T(1,128)S(1)}, s32[1,32]{1,0:T(1,128)}, u32[]{:S(2)}) %copy-start.3) | copy-done | bytes 152
  1.5 0.1 broadcast_in_dim.8.len_ref
  1.6 0.0 copy-start
  1.6 1.0 %copy-done = bf16[1,45,32,128]{3,2,1,0:T(8,128)(2,1)S(1)} copy-done((bf16[1,45,32,128]{3,2,1,0:T(8,128)(2,1)S(1)}, bf16[1,45,32,128]{3,2,1,0:T(8,128)(2,1)}, u32[]{:S(2)}) %copy-start) | copy-done | bytes 368664
  2.6 0.0 copy-start.1
  2.6 0.9 %copy-done.1 = bf16[32,32,128]{2,1,0:T(8,128)(2,1)S(1)} copy-done((bf16[32,32,128]{2,1,0:T(8,128)(2,1)S(1)}, bf16[32,32,128]{2,1,0:T(8,128)(2,1)}, u32[]{:S(2)}) %copy-start.1) | copy-done | bytes 262168
  3.6 36.1 %shard_map.46 = f32[4,8,128]{2,1,0:T(8,128)S(1)} custom-call(bf16[45,32,128]{2,1,0:T(8,128)(2,1)S(1)} %bitcast.13, bf16[4,256,128]{2,1,0:T(8,128)(2,1)S(1)} %bitcast.14, s32[32,128]{1,0:T(8,128)S(1)} %broadcast_in_dim.8.len_ref, s32[4,128]{1,0:T(4,128)S(1)} %reshape.25.cand_ref), custom_call_target="tpu_custom_call" | custom-call | tf_op jit(solution)/shard_map/pallas_call | solution.py:371
  39.6 0.1 copy.11
  39.8 0.7 %copy.10 = f32[32,4,8]{0,2,1:T(8,128)} copy(f32[32,4,8]{2,0,1:T(8,128)S(1)} %bitcast.16) | data formatting | bytes 8192 | tf_op jit(solution)/shard_map/reshape | solution.py:404
  (3 shorter events, 0.0 us)
Async XLA Ops:
  0.0 0.7 %copy-start.2 = (s32[32,4]{0,1:T(4,128)S(1)}, s32[32,4]{0,1:T(4,128)}, u32[]{:S(2)}) copy-start(s32[32,4]{0,1:T(4,128)} %param.5) | copy-start | bytes 1540
  0.9 0.7 %copy-start.3 = (s32[1,32]{1,0:T(1,128)S(1)}, s32[1,32]{1,0:T(1,128)}, u32[]{:S(2)}) copy-start(s32[1,32]{1,0:T(1,128)} %param.7) | copy-start | bytes 388
  1.6 1.0 %copy-start = (bf16[1,45,32,128]{3,2,1,0:T(8,128)(2,1)S(1)}, bf16[1,45,32,128]{3,2,1,0:T(8,128)(2,1)}, u32[]{:S(2)}) copy-start(bf16[1,45,32,128]{3,2,1,0:T(8,128)(2,1)} %param.6) | copy-start | bytes 1105924
  2.6 0.9 %copy-start.1 = (bf16[32,32,128]{2,1,0:T(8,128)(2,1)S(1)}, bf16[32,32,128]{2,1,0:T(8,128)(2,1)}, u32[]{:S(2)}) copy-start(bf16[32,32,128]{2,1,0:T(8,128)(2,1)} %param.4) | copy-start | bytes 786436

commit v2 on v1

--- a/solution.py
+++ b/solution.py
@@ -93,8 +93,9 @@
 ):
     slots = p_ref.shape[0]
     piece = slots // chunks
-    cols = q_len and q_all.shape[1]
+    cols = q_all.shape[1]
     tiles = cols // LANES
+    per = LANES // q_len
     cand_count = cand_ref.shape[0]
     depth = owners // 2
     me, part = lax.axis_index("blk"), lax.axis_index("tok")
@@ -116,19 +117,41 @@
     own_p.start()
 
     barrier = pltpu.get_barrier_semaphore()
-    total = owners * parts
-    flat = me * parts + part
-
-    def greet(i, carry):
-        other = (flat + i) % total
+
+    def greet(blk, tok):
         pl.semaphore_signal(
-            barrier, inc=1, device_id={"blk": other // parts, "tok": other % parts},
-            device_id_type=MESH,
-        )
-        return carry
-
-    lax.fori_loop(1, total, greet, 0)
-    pl.semaphore_wait(barrier, total - 1)
+            barrier, inc=1, device_id={"blk": blk, "tok": tok}, device_id_type=MESH
+        )
+
+    def in_column(j):
+        return (z + j) % depth * 2 + y
+
+    for j in range(1, depth):
+        greet(in_column(j), part)
+    greet(z * 2 + 1 - y, part)
+    for j in range(1, parts):
+        greet(me, (part + j) % parts)
+
+    def query_of(at):
+        rest = at % q_len
+        query = rest // tiles * (tiles * per) + rest % tiles * per + at // q_len
+        return jnp.where(rest < parts * tiles, query, -1)
+
+    queries = cand_ref.shape[1]
+    place = lax.broadcasted_iota(jnp.int32, (queries, LANES), 0)
+    spread = place == query_of(lax.broadcasted_iota(jnp.int32, (queries, LANES), 1))
+    cand = jnp.dot(
+        cand_ref[...].astype(jnp.float32).astype(jnp.bfloat16),
+        spread.astype(jnp.float32).astype(jnp.bfloat16),
+        preferred_element_type=jnp.float32,
+    )
+    place = lax.broadcasted_iota(jnp.int32, (width, width), 0)
+    same = place == lax.broadcasted_iota(jnp.int32, (width, width), 1)
+    counts = jnp.broadcast_to(len_ref[...].astype(jnp.float32), (width, width))
+    limit = jnp.sum(jnp.where(same, counts, 0.0), axis=1, keepdims=True)
+    limit = jnp.broadcast_to(limit, (width, LANES))
+
+    pl.semaphore_wait(barrier, depth - 1 + 1 + parts - 1)
 
     def q_copy(src, slot, way, blk):
         return remote(src, q_all.at[slot], q_send.at[slot, way], q_recv.at[slot], blk, part)
@@ -157,11 +180,8 @@
     def beside(slot, src):
         return q_copy(src, slot, 0, z * 2 + 1 - y)
 
-    def along(slot, src, to_z):
-        return q_copy(src, slot, 1, to_z * 2 + y)
-
-    def along_down(slot, src):
-        return q_copy(src, slot, 2, (z - 1) * 2 + y)
+    def along(j):
+        return q_copy(q_ref.at[part], me, j, in_column(j))
 
     @pl.when(part == 0)
     def _():
@@ -170,14 +190,8 @@
             first_copy(j).start()
 
     beside(me, q_ref.at[part]).start()
-
-    @pl.when(z + 1 < depth)
-    def _():
-        along(me, q_ref.at[part], z + 1).start()
-
-    @pl.when(z > 0)
-    def _():
-        along_down(me, q_ref.at[part]).start()
+    for j in range(1, depth):
+        along(j).start()
 
     near.start()
     for i in range(chunks):
@@ -204,7 +218,7 @@
 
     def fix(place, tok):
         pos = lax.broadcasted_iota(jnp.int32, (slots, width, LANES), 0) + tok * slots
-        kept = pos < len_ref[...][None]
+        kept = pos.astype(jnp.float32) < limit[None]
         mine = p_all[place].astype(jnp.float32)
         first = p_first[...].astype(jnp.float32)
         p_fix[place] = jnp.where(kept, mine, first[None]).astype(p_fix.dtype)
@@ -222,46 +236,30 @@
     near.wait_recv()
     fix(1, partner)
 
-    def onward(n):
+    def arrive(n):
         slot = slot_of(n)
-        from_z = slot // 2
         src = q_all.at[slot]
-        up = (from_z < z) & (z + 1 < depth)
-        down = (from_z > z) & (z > 0)
-        return slot, src, up, down
-
-    def early(n, carry):
-        slot, src, up, down = onward(n)
         pltpu.make_async_copy(src, src, q_recv.at[slot]).wait()
 
         @pl.when(is_column(n) & (n > 0))
         def _():
             beside(slot, src).start()
 
-            @pl.when(up)
-            def _():
-                along(slot, src, z + 1).start()
-
-            @pl.when(down)
-            def _():
-                along_down(slot, src).start()
-
+        return slot
+
+    half = owners // 2
+
+    def early(n, carry):
+        slot = arrive(n)
         for i in range(chunks):
 
-            @pl.when(n == 2 * i + 2)
+            @pl.when(n == min(i + 1, half - 1))
             def _():
                 far_copy(i).wait_recv()
                 hop_copy(i).start()
 
         acc[n] = jnp.maximum(best(slot, 0), best(slot, 1))
         return carry
-
-    lax.fori_loop(0, owners, early, 0)
-
-    for i in range(chunks):
-        hop_copy(i).wait_recv()
-    fix(2, opposite)
-    fix(3, diagonal)
 
     lane = lax.broadcasted_iota(jnp.int32, (SUB, LANES), 1)
 
@@ -271,7 +269,7 @@
             r_out.at[slot], r_in.at[me, part], r_send.at[slot, tok], r_recv.at[me, part], slot, tok
         )
 
-    def late(n, carry):
+    def late(n):
         slot = slot_of(n)
         found = jnp.maximum(acc[n], jnp.maximum(best(slot, 2), best(slot, 3)))
         tile = jnp.zeros((SUB, LANES), jnp.float32)
@@ -299,24 +297,34 @@
         def _():
             r_in[me, part] = tile
 
+    lax.fori_loop(0, half, early, 0)
+    for i in range(chunks):
+        hop_copy(i).wait_recv()
+    fix(2, opposite)
+    fix(3, diagonal)
+
+    def both(i, carry):
+        n = lax.select(i % 2 == 1, half + i // 2, i // 2)
+
+        @pl.when(i % 2 == 1)
+        def _():
+            slot = arrive(n)
+            acc[n] = jnp.maximum(best(slot, 0), best(slot, 1))
+
+        late(n)
         return carry
 
-    lax.fori_loop(0, owners, late, 0)
+    lax.fori_loop(0, owners, both, 0)
+
+    for j in range(1, depth):
+        along(j).wait_send()
 
     def drain(n, carry):
-        slot, src, up, down = onward(n)
+        slot = slot_of(n)
 
         @pl.when(is_column(n))
         def _():
-            beside(slot, src).wait_send()
-
-            @pl.when(up | ((n == 0) & (z + 1 < depth)))
-            def _():
-                along(slot, src, z + 1).wait_send()
-
-            @pl.when(down | ((n == 0) & (z > 0)))
-            def _():
-                along_down(slot, src).wait_send()
+            beside(slot, q_all.at[slot]).wait_send()
 
         for j in range(parts):
 
@@ -347,9 +355,15 @@
             moved = pltpu.roll(r_in[blk, tok], (tiles * (tok - part) + LANES) % LANES, 1)
             merged = jnp.where((lane % q_len) // tiles == tok, moved, merged)
         for k in range(cand_count):
-            picked[k] = jnp.where(cand_ref[k : k + 1, :] == blk, merged, picked[k])
+            picked[k] = jnp.where(cand[k : k + 1, :] == blk, merged, picked[k])
+    at = lax.broadcasted_iota(jnp.int32, (LANES, queries), 0)
+    gather = query_of(at) == lax.broadcasted_iota(jnp.int32, (LANES, queries), 1)
+    rows = jnp.dot(
+        jnp.concatenate(picked, axis=0), gather.astype(jnp.float32),
+        precision=lax.Precision.HIGHEST, preferred_element_type=jnp.float32,
+    )
     for k in range(cand_count):
-        out_ref[k] = picked[k]
+        out_ref[k] = rows[k * SUB : (k + 1) * SUB]
 
 
 def dense_shards(queries, candidates, passages, lengths):
@@ -359,18 +373,11 @@
     slots, width = passages.shape[1], passages.shape[2]
     share = query_count // parts
     cols = share * q_len
-    tiles = cols // LANES
-    per = LANES // q_len
     chunks = 3 if slots % 3 == 0 else 1
-    used = parts * tiles
-    cand = candidates.reshape(parts, tiles, per, cand_count).transpose(3, 2, 0, 1)
-    cand = cand.reshape(cand_count, per, used)
-    cand = jnp.pad(cand, ((0, 0), (0, 0), (0, q_len - used))).reshape(cand_count, LANES)
-    limits = jnp.broadcast_to(lengths[0][:, None], (width, LANES))
     dma = pltpu.SemaphoreType.DMA
     out = pl.pallas_call(
         functools.partial(dense_kernel, owners, parts, width, q_len, chunks),
-        out_shape=jax.ShapeDtypeStruct((cand_count, SUB, LANES), jnp.float32),
+        out_shape=jax.ShapeDtypeStruct((cand_count, SUB, query_count), jnp.float32),
         in_specs=[pl.BlockSpec(memory_space=pl.ANY)] * 2
         + [pl.BlockSpec(memory_space=pltpu.VMEM)] * 2,
         out_specs=pl.BlockSpec(memory_space=pltpu.VMEM),
@@ -382,7 +389,7 @@
             pltpu.VMEM((owners, width, cols), jnp.float32),
             pltpu.VMEM((owners, SUB, LANES), jnp.float32),
             pltpu.VMEM((owners, parts, SUB, LANES), jnp.float32),
-            dma((owners, 3)),
+            dma((owners, owners // 2)),
             dma((owners,)),
             dma,
             dma((2,)),
@@ -396,12 +403,10 @@
             dma((owners, parts)),
         ],
         compiler_params=pltpu.CompilerParams(
-            collective_id=0, has_side_effects=True, vmem_limit_bytes=48 * 1024 * 1024
+            collective_id=0, has_side_effects=True, vmem_limit_bytes=60 * 1024 * 1024
         ),
-    )(passages[0], queries.reshape(parts, cols, dim), limits, cand)
-    out = out.reshape(cand_count, SUB, per, q_len)[:, :, :, :used]
-    out = out.reshape(cand_count, SUB, per, parts, tiles).transpose(3, 4, 2, 0, 1)
-    return out.reshape(query_count, cand_count, SUB)
+    )(passages[0], queries.reshape(parts, cols, dim), lengths, candidates.T)
+    return out.transpose(2, 0, 1)
 
 
 def dense_fits(mesh, queries, candidates, passages):

time: 40.7 us -> 35.2 us (0.86)
  local copies, waits for them, and re-layouts: 4.38 us -> 1.32 us
  Pallas kernels: 36.1 us -> 33.5 us
    pallas_call x1, Pallas kernels: 36.1 us -> 33.5 us  [dense_shards(): pl.pallas_call(functools.partial(dense_kernel, owners, parts, width, q_le...]
    unnamed x9 -> x1, local copies, waits for them, and re-layouts: 3.29 us -> 1.32 us
    reshape x4 -> x0, local copies, waits for them, and re-layouts: 0.98 us -> none  [the longest x1 0.68 us: dense_shards(): return out.reshape(query_count, cand_count, SUB)]
where the time goes in v2:
time: 35.2 us; the launch traced here: 34.8 us
  Pallas kernels  33.5 us (95%)
  local copies, waits for them, and re-layouts  1.32 us (4%)
    pallas_call x1, Pallas kernels, dense_shards(): pl.pallas_call(functools.partial(dense_kernel, owners, parts, width, q_le...  33.5 us
    unnamed x1, local copies, waits for them, and re-layouts  1.32 us

profile of v2, /device:TPU:0, one launch (start us, length us, event | category | flops | bytes accessed | tf_op | source)
XLA Modules:
  0.0 34.8 jit_solution(13019750356885921216)
XLA Ops:
  0.0 33.5 %shard_map.46 = f32[4,8,32]{2,1,0:T(8,128)} custom-call(bf16[45,32,128]{2,1,0:T(8,128)(2,1)} %bitcast.4, bf16[4,256,128]{2,1,0:T(8,128)(2,1)} %bitcast.5, s32[1,32]{1,0:T(1,128)} %len_ref.1, s32[4,32]{1,0:T(4,128)} %bitcast.7), custom_call_target="tpu_custom_call" | custom-call | tf_op jit(solution)/shard_map/pallas_call | solution.py:378
  33.5 1.3 %copy.6 = f32[32,4,8]{0,2,1:T(8,128)} copy(f32[32,4,8]{0,2,1:T(8,128)} %bitcast.6) | data formatting | bytes 8192
